TPU v7x, 512 devices: a whole 4x8x8 slice. The times are simulated.
512 devices in a mesh: tm: 8 (over x, core), seq: 64 (over y, z).
Axes of the slice: x: 4, y: 8, z: 8, core: 2. Of those that a mesh axis runs over, the one named last changes fastest.
Arguments:
- latents: bfloat16 [8, 1024, 4096], P('tm', 'seq'), may hold values from -14 to 14
- end_latent: bfloat16 [1024, 4096], P('seq'), may hold values from -14 to 14
- timesteps: int32 [9], replicated, may hold values from 0 to 1000, as said below
- modulation: float32 [8, 3, 4096], P('tm'), may hold values from -10 to 10
- proj_weight: bfloat16 [3, 32, 128, 128], replicated, may hold values from -1 to 1
Outputs:
- new_latents: bfloat16 [8, 1024, 4096], P('tm', 'seq')
- update_error: float32 [8, 1024], P('tm', 'seq')
Inputs may be any that keep to these rules, and one draw needn't show every extreme that they name: `timesteps`: strictly decreasing.
All inputs are finite; a program needn't handle non-finite values.
Results may differ from a plain program's by a relative error of at most 0.0065.
Values may be sent and summed in bfloat16 or wider, within the bound.
No kernel may reach another device: no remote copies, remote signals or barrier semaphores. Data moves between devices by JAX's collectives and lax.ppermute only.
A program may use at most 64 MiB of HBM per device.

v0:
```python
import math

import jax
import jax.numpy as jnp
from jax import lax
from jax.sharding import PartitionSpec as P


def prefix(shard, axis, join, neutral):
    place = lax.axis_index(axis)
    gathered = lax.all_gather(shard.astype(jnp.bfloat16), axis)
    state = jnp.zeros_like(shard) + jnp.asarray(neutral, shard.dtype)

    def one(lap, state):
        return join(state, lax.dynamic_index_in_dim(gathered, lap, 0, False).astype(shard.dtype))

    return lax.fori_loop(0, place, one, state)


def from_root(block, axis, source):
    block = jnp.where(lax.axis_index(axis) == source, block, jnp.zeros_like(block))
    return lax.psum(block, axis)


def passed_along(shard, axis, by):
    peers = lax.axis_size(axis)
    pairs = [(i, i + by) for i in range(peers) if 0 <= i + by < peers]
    return lax.ppermute(shard, axis, pairs)


def sigmas_of(timesteps):
    frac = timesteps.astype(jnp.float32) / 1000.0
    return 5.0 * frac / (1.0 + 4.0 * frac)


def add_terms(earlier, later):
    return earlier + later


def project(block, weight):
    return jnp.einsum("rhd,hde->rhe", block, weight, preferred_element_type=jnp.float32).astype(
        jnp.bfloat16
    )


def body(latents, end_latent, timesteps, modulation, proj_weight):
    group = lax.axis_size("seq")
    heads = proj_weight.shape[1]
    head_size = proj_weight.shape[2]
    rows = latents.shape[1]
    qsplit = max(1, group // heads)
    heads_dev = max(1, heads // group)
    part_rows = rows // qsplit
    time_index = lax.axis_index("tm")
    own_latent = latents[0]
    factors = modulation[0]
    modulated = (own_latent.astype(jnp.float32) * (1.0 + factors[1]) + factors[0]).astype(
        jnp.bfloat16
    )
    modulated = modulated.reshape(rows, heads, head_size)

    def spread(block):
        return jnp.repeat(block, qsplit, axis=1).reshape(
            block.shape[0], group, heads_dev, head_size
        )

    query_all = project(modulated, proj_weight[0])
    key_all = project(modulated, proj_weight[1])
    value_all = project(modulated, proj_weight[2])
    shaped = query_all.reshape(qsplit, part_rows, group // qsplit, heads_dev, head_size)
    query = lax.all_to_all(
        shaped.transpose(1, 2, 0, 3, 4).reshape(part_rows, group, heads_dev, head_size),
        "seq",
        split_axis=1,
        concat_axis=0,
        tiled=True,
    ).reshape(group * part_rows, heads_dev, head_size)
    key_rows = lax.all_to_all(
        spread(key_all), "seq", split_axis=1, concat_axis=0, tiled=True
    ).reshape(group * rows, heads_dev, head_size)
    values = lax.all_to_all(
        spread(value_all), "seq", split_axis=1, concat_axis=0, tiled=True
    ).reshape(group * rows, heads_dev, head_size)
    total_rows = query.shape[0]
    block_rows = math.gcd(total_rows, 512)
    scale_factor = 1.0 / math.sqrt(head_size)

    def attend_block(block):
        scores = (
            jnp.einsum("qhd,khd->hqk", block, key_rows, preferred_element_type=jnp.float32)
            * scale_factor
        )
        row_max = jnp.max(scores, axis=-1, keepdims=True)
        probs = jnp.exp(scores - row_max)
        row_total = jnp.sum(probs, axis=-1, keepdims=True)
        mixed = (
            jnp.einsum(
                "hqk,khd->hqd",
                probs.astype(jnp.bfloat16),
                values,
                preferred_element_type=jnp.float32,
            )
            / row_total
        )
        return mixed.transpose(1, 0, 2).astype(jnp.bfloat16)

    blocks = query.reshape(total_rows // block_rows, block_rows, heads_dev, head_size)
    attended = lax.map(attend_block, blocks).reshape(total_rows, 1, heads_dev, head_size)
    returned = lax.all_to_all(attended, "seq", split_axis=0, concat_axis=1, tiled=True)
    attention = returned.reshape(part_rows, group // qsplit, qsplit, heads_dev, head_size)
    attention = attention.transpose(2, 0, 1, 3, 4).reshape(rows, heads * head_size)
    sigmas = sigmas_of(timesteps)
    bounds_pair = lax.dynamic_slice_in_dim(sigmas, time_index, 2)
    step_size = bounds_pair[1] - bounds_pair[0]
    drift = step_size * factors[2] * attention.astype(jnp.float32)
    earlier = prefix(drift, "tm", add_terms, jnp.zeros_like(drift))
    first = from_root(own_latent, "tm", 0)
    updated = first.astype(jnp.float32) + earlier + drift
    ahead = passed_along(own_latent, "tm", -1)
    old_next = jnp.where(time_index == lax.axis_size("tm") - 1, end_latent, ahead)
    update_error = jnp.mean((updated - old_next.astype(jnp.float32)) ** 2, axis=-1)
    return (updated.astype(jnp.bfloat16)[None], update_error[None])


def solution(mesh):
    placed = (P("tm", "seq", None), P("seq", None), P(), P("tm", None, None), P())
    return jax.shard_map(
        body,
        mesh=mesh,
        in_specs=placed,
        out_specs=(P("tm", "seq", None), P("tm", "seq")),
        check_vma=False,
    )
```

profile of v0, /device:TPU:1, one launch (start us, length us, event | category | flops | bytes accessed | tf_op | source)
XLA Modules:
  0.0 201.9 jit_solution(283698694933814755)
XLA Ops:
  7.2 0.7 add_divide_fusion
  8.5 0.9 convert_bitcast_fusion
  10.7 0.8 slice_multiply_fusion
  11.7 2.3 %convolution_convert_fusion.2 = bf16[32,16,128]{2,1,0:T(8,128)(2,1)} fusion(bf16[16,32,128]{2,0,1:T(8,128)(2,1)S(1)} %fusion.18, bf16[3,32,128,128]{3,2,1,0:T(8,128)(2,1)} %param.11), kind=kOutput, calls=%fused_computation.8 | convolution fusion | flops 16842752 | bytes 1310720 | tf_op jit(solution)/shard_map/rhd,hde->rhe/dot_general | solution.py:41
  13.9 17.1 %all-to-all-start = ((bf16[8,64,1,128]{3,0,2,1:T(8,128)(2,1)}), bf16[8,64,1,128]{3,0,2,1:T(8,128)(2,1)S(1)}, u32[]{:S(2)}, u32[]{:S(2)}) async-start(bf16[8,64,1,128]{3,0,2,1:T(8,128)(2,1)} %bitcast.10), calls=%async_computation | async-start | bytes 262144 | tf_op jit(solution)/shard_map/all_to_all | solution.py:71
  31.1 1.6 fusion.3
  32.7 9.9 %all-to-all-done = bf16[8,64,1,128]{3,0,2,1:T(8,128)(2,1)S(1)} async-done(((bf16[8,64,1,128]{3,0,2,1:T(8,128)(2,1)}), bf16[8,64,1,128]{3,0,2,1:T(8,128)(2,1)S(1)}, u32[]{:S(2)}, u32[]{:S(2)}) %all-to-all-start) | async-done | bytes 131104 | tf_op jit(solution)/shard_map/all_to_all | solution.py:71
  42.6 0.7 broadcast_in_dim.28
  43.3 4.6 %all-to-all-start.1 = ((bf16[16,64,1,128]{3,0,2,1:T(8,128)(2,1)}), bf16[16,64,1,128]{3,0,2,1:T(8,128)(2,1)S(1)}, u32[]{:S(2)}, u32[]{:S(2)}) async-start(bf16[16,64,1,128]{3,0,2,1:T(8,128)(2,1)} %bitcast.16), calls=%async_computation.1 | async-start | bytes 524288 | tf_op jit(solution)/shard_map/all_to_all | solution.py:78
  47.9 1.6 fusion.4
  49.5 11.0 %all-to-all-done.1 = bf16[16,64,1,128]{3,0,2,1:T(8,128)(2,1)S(1)} async-done(((bf16[16,64,1,128]{3,0,2,1:T(8,128)(2,1)}), bf16[16,64,1,128]{3,0,2,1:T(8,128)(2,1)S(1)}, u32[]{:S(2)}, u32[]{:S(2)}) %all-to-all-start.1) | async-done | bytes 262176 | tf_op jit(solution)/shard_map/all_to_all | solution.py:78
  60.5 0.7 broadcast_in_dim.29
  61.2 4.6 %all-to-all-start.2 = ((bf16[16,64,1,128]{3,0,2,1:T(8,128)(2,1)}), bf16[16,64,1,128]{3,0,2,1:T(8,128)(2,1)S(1)}, u32[]{:S(2)}, u32[]{:S(2)}) async-start(bf16[16,64,1,128]{3,0,2,1:T(8,128)(2,1)} %bitcast.22), calls=%async_computation.2 | async-start | bytes 524288 | tf_op jit(solution)/shard_map/all_to_all | solution.py:81
  66.9 11.5 %all-to-all-done.2 = bf16[16,64,1,128]{3,0,2,1:T(8,128)(2,1)S(1)} async-done(((bf16[16,64,1,128]{3,0,2,1:T(8,128)(2,1)}), bf16[16,64,1,128]{3,0,2,1:T(8,128)(2,1)S(1)}, u32[]{:S(2)}, u32[]{:S(2)}) %all-to-all-start.2) | async-done | bytes 262176 | tf_op jit(solution)/shard_map/all_to_all | solution.py:81
  79.5 0.7 reduce.4
  80.2 15.4 %all_to_all.57 = bf16[64,2,512]{2,1,0:T(2,128)(2,1)S(1)} all-to-all(bf16[64,2,512]{2,1,0:T(2,128)(2,1)S(1)} %reshape.162), channel_id=1, replica_groups=mesh['tm'=8,'seq'=64] {'seq'}, dimensions={0} | all-to-all | bytes 262144 | tf_op jit(solution)/shard_map/all_to_all | solution.py:109
  96.0 0.7 fusion.16
  96.8 7.5 %collective-permute-start = (bf16[16,4096]{1,0:T(8,128)(2,1)S(1)}, bf16[16,4096]{1,0:T(8,128)(2,1)S(1)}, u32[]{:S(2)}, u32[]{:S(2)}) collective-permute-start(bf16[16,4096]{1,0:T(8,128)(2,1)S(1)} %bitcast.91), channel_id=1, source_target_pairs={{64,0},{128,64},{192,128},{256,192},{320,256},{384,320},{448,384},... | collective-permute-start | bytes 393224 | tf_op jit(solution)/shard_map/ppermute | solution.py:28
  104.3 0.7 broadcast_select_fusion
  105.0 17.6 %all-gather.2.cloned.1.call-done = bf16[8,16,4096]{2,1,0:T(8,128)(2,1)} async-done(((bf16[1,16,4096]{2,1,0:T(8,128)(2,1)}), bf16[8,16,4096]{2,1,0:T(8,128)(2,1)}) %all-gather.2.cloned.1.call-update) | async-done | bytes 1048592 | tf_op jit(solution)/shard_map/all_gather | solution.py:11
  122.6 1.0 while.2
  122.7 0.9 convert_add_fusion.2
  123.6 69.1 %all-reduce.2.cloned.1.call-done = bf16[16,4096]{1,0:T(8,128)(2,1)} async-done(((bf16[16,4096]{1,0:T(8,128)(2,1)}), bf16[16,4096]{1,0:T(8,128)(2,1)}) %all-reduce.2.cloned.1.call-update) | async-done | bytes 131088 | tf_op jit(solution)/shard_map/psum | solution.py:22
  192.8 1.8 multiply_reduce_fusion.1
  (22 shorter events, 4.1 us)
Async XLA Ops:
  13.9 28.6 %all-to-all-start = ((bf16[8,64,1,128]{3,0,2,1:T(8,128)(2,1)}), bf16[8,64,1,128]{3,0,2,1:T(8,128)(2,1)S(1)}, u32[]{:S(2)}, u32[]{:S(2)}) async-start(bf16[8,64,1,128]{3,0,2,1:T(8,128)(2,1)} %bitcast.10), calls=%async_computation | async-start | bytes 262144 | tf_op jit(solution)/shard_map/all_to_all | solution.py:71
  43.3 17.2 %all-to-all-start.1 = ((bf16[16,64,1,128]{3,0,2,1:T(8,128)(2,1)}), bf16[16,64,1,128]{3,0,2,1:T(8,128)(2,1)S(1)}, u32[]{:S(2)}, u32[]{:S(2)}) async-start(bf16[16,64,1,128]{3,0,2,1:T(8,128)(2,1)} %bitcast.16), calls=%async_computation.1 | async-start | bytes 524288 | tf_op jit(solution)/shard_map/all_to_all | solution.py:78
  61.2 17.2 %all-to-all-start.2 = ((bf16[16,64,1,128]{3,0,2,1:T(8,128)(2,1)}), bf16[16,64,1,128]{3,0,2,1:T(8,128)(2,1)S(1)}, u32[]{:S(2)}, u32[]{:S(2)}) async-start(bf16[16,64,1,128]{3,0,2,1:T(8,128)(2,1)} %bitcast.22), calls=%async_computation.2 | async-start | bytes 524288 | tf_op jit(solution)/shard_map/all_to_all | solution.py:81
  65.9 56.7 %all-gather.2.cloned.1.call-start = ((), (), s32[]{:S(2)}) async-start(), calls=%async_computation.5 | async-start | bytes 1179648 | tf_op jit(solution)/shard_map/all_gather | solution.py:11
  78.4 18.3 %copy-start = (bf16[1,16,4096]{2,1,0:T(8,128)(2,1)S(1)}, bf16[1,16,4096]{2,1,0:T(8,128)(2,1)}, u32[]{:S(2)}) copy-start(bf16[1,16,4096]{2,1,0:T(8,128)(2,1)} %param.7) | copy-start | bytes 393220
  96.7 96.1 %copy-start.1 = (bf16[16,4096]{1,0:T(8,128)(2,1)S(1)}, bf16[16,4096]{1,0:T(8,128)(2,1)}, u32[]{:S(2)}) copy-start(bf16[16,4096]{1,0:T(8,128)(2,1)} %param.8) | copy-start | bytes 393220
  96.7 96.1 %all-reduce.2.cloned.1.call-start = ((), (), s32[]{:S(2)}) async-start(), calls=%async_computation.4 | async-start | bytes 262144 | tf_op jit(solution)/shard_map/psum | solution.py:22
  96.8 96.0 %collective-permute-start = (bf16[16,4096]{1,0:T(8,128)(2,1)S(1)}, bf16[16,4096]{1,0:T(8,128)(2,1)S(1)}, u32[]{:S(2)}, u32[]{:S(2)}) collective-permute-start(bf16[16,4096]{1,0:T(8,128)(2,1)S(1)} %bitcast.91), channel_id=1, source_target_pairs={{64,0},{128,64},{192,128},{256,192},{320,256},{384,320},{448,384},... | collective-permute-start | bytes 393224 | tf_op jit(solution)/shard_map/ppermute | solution.py:28
Sparse Core Ops, SparseCore 0:
  96.8 25.7 all-gather.1
  124.9 67.7 all-reduce.1
where the time goes:
time: 203 us; the launch traced here: 202 us
  waiting for transfers between devices  119 us (59%)
  starting transfers between devices  34 us (17%)
  blocking collectives  15.4 us (8%)
  between operations  15.4 us (8%)
  other arithmetic  8.58 us (4%)
  matrix products  6.5 us (3%)
  local copies, waits for them, and re-layouts  2.87 us (1%)
    psum x1, waiting for transfers between devices, from_root(): return lax.psum(block, axis)  69.1 us
    all_gather x1, waiting for transfers between devices, prefix(): gathered = lax.all_gather(shard.astype(jnp.bfloat16), axis)  17.6 us
    all_to_all x1, starting transfers between devices, body(): lax.all_to_all(shaped.transpose(1, 2, 0, 3, 4).reshape(part_rows, group,...  17.1 us
    all_to_all x1, blocking collectives, body(): lax.all_to_all(attended, 'seq', split_axis=0, concat_axis=1, tiled=True)  15.4 us
    all_to_all x1, waiting for transfers between devices, body(): lax.all_to_all(spread(value_all), 'seq', split_axis=1, concat_axis=0, til...  11.5 us
    all_to_all x1, waiting for transfers between devices, body(): lax.all_to_all(spread(key_all), 'seq', split_axis=1, concat_axis=0, tiled...  11 us
    all_to_all x1, waiting for transfers between devices, body(): lax.all_to_all(shaped.transpose(1, 2, 0, 3, 4).reshape(part_rows, group,...  9.91 us
    ppermute x1, starting transfers between devices, passed_along(): return lax.ppermute(shard, axis, pairs)  7.53 us
  transfers between devices with their start and end apart: 6, of which 5 were waited for; matrix products, arithmetic and copies ran while one was open for 3% of the time, Pallas kernels for 0%

commit v1 on v0

v1 whole, which is shorter than its diff:
```python
import math

import jax
import jax.numpy as jnp
from jax import lax
from jax.sharding import Mesh, PartitionSpec as P


def sigmas_of(timesteps):
    frac = timesteps.astype(jnp.float32) / 1000.0
    return 5.0 * frac / (1.0 + 4.0 * frac)


def attend(tokens, factors, weights, half):
    sources, rows, size = tokens.shape
    modulated = (tokens.astype(jnp.float32) * (1.0 + factors[1]) + factors[0]).astype(jnp.bfloat16)
    halves = modulated.reshape(sources, 2, rows // 2, size)
    own = jnp.where(half == 0, halves[:, 0], halves[:, 1]).reshape(sources * rows // 2, size)
    every = modulated.reshape(sources * rows, size)

    def project(block, weight):
        return jnp.dot(block, weight, preferred_element_type=jnp.float32).astype(jnp.bfloat16)

    query = project(own, weights[0])
    key = project(every, weights[1])
    value = project(every, weights[2])
    scores = lax.dot_general(
        query, key, (((1,), (1,)), ((), ())), preferred_element_type=jnp.float32
    ) * (1.0 / math.sqrt(size))
    probs = jnp.exp(scores - jnp.max(scores, axis=-1, keepdims=True))
    total = jnp.sum(probs, axis=-1, keepdims=True)
    mixed = jnp.dot(probs.astype(jnp.bfloat16), value, preferred_element_type=jnp.float32) / total
    return mixed.astype(jnp.bfloat16).reshape(sources, rows // 2, size)


def body(latents, end_latent, timesteps, modulation, proj_weight):
    heads, size = proj_weight.shape[1], proj_weight.shape[2]
    rows, width = latents.shape[1:]
    across, cores, group = lax.axis_size("x"), lax.axis_size("core"), lax.axis_size("seq")
    own_x, own_core, place = lax.axis_index("x"), lax.axis_index("core"), lax.axis_index("seq")
    time_index = own_x * cores + own_core
    copies = group // heads
    head, half = place // copies, place % copies
    own_latent = latents[0]

    window = lax.all_gather(own_latent, ("x", "core"))

    blocks = own_latent.reshape(rows, heads, size).transpose(1, 0, 2)
    sent = jnp.repeat(blocks, copies, axis=0)
    tokens = lax.all_to_all(sent, "seq", 0, 0, tiled=True)
    factors = lax.dynamic_index_in_dim(modulation[0].reshape(3, heads, size), head, 1, False)
    weights = lax.dynamic_index_in_dim(proj_weight, head, 1, False)
    mixed = attend(tokens, factors, weights, half)
    returned = lax.all_to_all(mixed, "seq", 0, 0, tiled=True)
    attention = returned.reshape(heads, copies, rows // copies, size).transpose(1, 2, 0, 3)
    attention = attention.reshape(rows, width).astype(jnp.float32)

    sigmas = sigmas_of(timesteps)
    pair = lax.dynamic_slice_in_dim(sigmas, time_index, 2)
    drift = (pair[1] - pair[0]) * modulation[0, 2] * attention
    spread = jnp.broadcast_to(drift.astype(jnp.bfloat16)[None], (across, rows, width))
    along = lax.all_to_all(spread, "x", 0, 0, tiled=True)
    before = (jnp.arange(across) < own_x)[:, None, None]
    earlier = jnp.sum(jnp.where(before, along.astype(jnp.float32), 0.0), axis=0)
    upto = earlier + drift
    pairs = lax.all_gather(jnp.where(own_core == 0, upto, earlier), "core")
    updated = window[0].astype(jnp.float32) + upto + jnp.where(own_core == 0, pairs[1], pairs[0])
    last = time_index == across * cores - 1
    ahead = lax.dynamic_index_in_dim(window, jnp.where(last, 0, time_index + 1), 0, False)
    old = jnp.where(last, end_latent, ahead).astype(jnp.float32)
    error = jnp.mean((updated - old) ** 2, axis=-1)
    return (updated.astype(jnp.bfloat16)[None], error[None])


def solution(mesh):
    inner = Mesh(mesh.devices.reshape(-1, 2, mesh.shape["seq"]), ("x", "core", "seq"))
    time = ("x", "core")
    return jax.shard_map(
        body,
        mesh=inner,
        in_specs=(P(time, "seq", None), P("seq", None), P(), P(time, None, None), P()),
        out_specs=(P(time, "seq", None), P(time, "seq")),
        check_vma=False,
    )
```

time: 203 us -> 96.3 us (0.47)
  waiting for transfers between devices: 119 us -> 25.6 us
  blocking collectives: 15.4 us -> 6.66 us
  starting transfers between devices: 34 us -> 27.1 us
  other arithmetic: 8.58 us -> 11.4 us
    psum x1 -> x0, waiting for transfers between devices: 69.1 us -> none  [from_root(): return lax.psum(block, axis)]
    all_gather x1, waiting for transfers between devices: 17.6 us -> 0.01 us  [body(): window = lax.all_gather(own_latent, ('x', 'core'))]
    all_to_all x1 -> x0, blocking collectives: 15.4 us -> none  [body(): lax.all_to_all(attended, 'seq', split_axis=0, concat_axis=1, tiled=True)]
    ppermute x1 -> x0, starting transfers between devices: 7.53 us -> none  [passed_along(): return lax.ppermute(shard, axis, pairs)]
    all_to_all x3, waiting for transfers between devices: 32.3 us -> 24.9 us  [the longest x1 10.8 us: body(): returned = lax.all_to_all(mixed, 'seq', 0, 0, tiled=True)]
    all_gather x0 -> x1, blocking collectives: none -> 6.66 us  [body(): pairs = lax.all_gather(jnp.where(own_core == 0, upto, earlier), 'core')]
    reduce_sum x2 -> x3, other arithmetic: 2.27 us -> 4.77 us  [the longest x1 2.08 us: attend(): total = jnp.sum(probs, axis=-1, keepdims=True)]
    dot_general x5 -> x3, matrix products: 6.5 us -> 6.18 us  [the longest x1 3.02 us: attend(): jnp.dot(probs.astype(jnp.bfloat16), value, preferred_element_type=jnp.flo...]
  transfers between devices with their start and end apart: 6 -> 4, of which waited for: 5 -> 3; matrix products, arithmetic and copies ran while one was open for 3% -> 16% of each run, Pallas kernels for 0% -> 0%
where the time goes in v1:
time: 96.3 us; the launch traced here: 95.7 us
  starting transfers between devices  27.1 us (28%)
  waiting for transfers between devices  25.6 us (27%)
  between operations  15.5 us (16%)
  other arithmetic  11.4 us (12%)
  blocking collectives  6.66 us (7%)
  matrix products  6.18 us (6%)
  local copies, waits for them, and re-layouts  3.36 us (3%)
    all_to_all x1, starting transfers between devices, body(): tokens = lax.all_to_all(sent, 'seq', 0, 0, tiled=True)  17.1 us
    all_to_all x1, waiting for transfers between devices, body(): returned = lax.all_to_all(mixed, 'seq', 0, 0, tiled=True)  10.8 us
    all_to_all x1, waiting for transfers between devices, body(): tokens = lax.all_to_all(sent, 'seq', 0, 0, tiled=True)  8.44 us
    all_gather x1, blocking collectives, body(): pairs = lax.all_gather(jnp.where(own_core == 0, upto, earlier), 'core')  6.66 us
    all_to_all x1, starting transfers between devices, body(): returned = lax.all_to_all(mixed, 'seq', 0, 0, tiled=True)  5.79 us
    all_to_all x1, waiting for transfers between devices, body(): along = lax.all_to_all(spread, 'x', 0, 0, tiled=True)  5.73 us
    all_to_all x1, starting transfers between devices, body(): along = lax.all_to_all(spread, 'x', 0, 0, tiled=True)  4.13 us
    dot_general x1, matrix products, attend(): jnp.dot(probs.astype(jnp.bfloat16), value, preferred_element_type=jnp.flo...  3.02 us
  transfers between devices with their start and end apart: 4, of which 3 were waited for; matrix products, arithmetic and copies ran while one was open for 16% of the time, Pallas kernels for 0%

profile of v1, /device:TPU:1, one launch (start us, length us, event | category | flops | bytes accessed | tf_op | source)
XLA Modules:
  0.0 95.7 jit_solution(9370525626059595251)
XLA Ops:
  7.2 1.1 %copy.13 = bf16[2,8,32,128]{3,2,1,0:T(8,128)(2,1)S(1)} copy(bf16[2,8,32,128]{3,1,2,0:T(8,128)(2,1)} %bitcast.90) | data formatting | bytes 262144
  8.3 0.7 broadcast_in_dim.13
  9.0 17.1 %all-to-all-start = ((bf16[64,16,128]{2,1,0:T(8,128)(2,1)}), bf16[64,16,128]{2,1,0:T(8,128)(2,1)S(1)}, u32[]{:S(2)}, u32[]{:S(2)}) async-start(bf16[64,16,128]{2,1,0:T(8,128)(2,1)} %bitcast.87), calls=%async_computation | async-start | bytes 524288 | tf_op jit(solution)/shard_map/all_to_all | solution.py:50
  26.2 0.7 all-gather.2.cloned.1.call-update
  27.0 0.7 add_divide_fusion
  27.7 0.6 fusion.32
  29.6 0.7 fusion.30
  30.3 8.4 %all-to-all-done = bf16[64,16,128]{2,1,0:T(8,128)(2,1)S(1)} async-done(((bf16[64,16,128]{2,1,0:T(8,128)(2,1)}), bf16[64,16,128]{2,1,0:T(8,128)(2,1)S(1)}, u32[]{:S(2)}, u32[]{:S(2)}) %all-to-all-start) | async-done | bytes 262176 | tf_op jit(solution)/shard_map/all_to_all | solution.py:50
  39.0 0.8 add_convert_fusion
  39.8 3.0 %multiply_reduce_fusion = (f32[512]{0:T(512)S(1)}, f32[512,1024]{1,0:T(8,128)}) fusion(bf16[512,128]{1,0:T(8,128)(2,1)S(1)} %convolution_convert_fusion.2, bf16[1024,128]{1,0:T(8,128)(2,1)} %bitcast.88, bf16[3,32,128,128]{3,2,1,0:T(8,128)(2,1)S(1)} %copy-done, s32[]{:T(128)S(6)} %add.90, s32[]{:T(128)S(6)} %select_n.79), kind=kOutput, calls=%fused_computation.1 | convolution fusion | flops 168951296 | bytes 2525192 | tf_op jit(solution)/shard_map/dot_general | solution.py:27
  42.8 2.1 %fusion = f32[512]{0:T(512)S(1)} fusion(f32[512,1024]{1,0:T(8,128)} %get-tuple-element.7, f32[512]{0:T(512)S(1)} %get-tuple-element.6), kind=kLoop, calls=%fused_computation.2 | loop fusion | flops 1572352 | bytes 2101248 | tf_op jit(solution)/shard_map/reduce_sum | solution.py:31
  44.8 3.0 %fusion.6 = bf16[64,8,128]{2,1,0:T(8,128)(2,1)} fusion(bf16[1024,128]{1,0:T(8,128)(2,1)S(1)} %bitcast.89, f32[512,1024]{1,0:T(8,128)} %get-tuple-element.7, f32[512]{0:T(512)S(1)} %get-tuple-element.6, f32[512]{0:T(512)S(1)} %fusion, bf16[3,32,128,128]{3,2,1,0:T(8,128)(2,1)S(1)} %copy-done, s32[]{:T(128)S(6)} %add.92, s32[]{:T(128)S(6)} %select_n.79), kind=kOutput, calls=%fused_computation.11 | convolution fusion | flops 169607168 | bytes 2527240 | tf_op jit(solution)/shard_map/dot_general | solution.py:32
  47.9 5.8 %all-to-all-start.1 = ((bf16[64,8,128]{2,1,0:T(8,128)(2,1)}), bf16[64,8,128]{2,1,0:T(8,128)(2,1)S(1)}, u32[]{:S(2)}, u32[]{:S(2)}) async-start(bf16[64,8,128]{2,1,0:T(8,128)(2,1)} %fusion.6), calls=%async_computation.1 | async-start | bytes 262144 | tf_op jit(solution)/shard_map/all_to_all | solution.py:54
  53.7 0.7 slice_multiply_fusion
  54.4 10.8 %all-to-all-done.1 = bf16[64,8,128]{2,1,0:T(8,128)(2,1)S(1)} async-done(((bf16[64,8,128]{2,1,0:T(8,128)(2,1)}), bf16[64,8,128]{2,1,0:T(8,128)(2,1)S(1)}, u32[]{:S(2)}, u32[]{:S(2)}) %all-to-all-start.1) | async-done | bytes 131104 | tf_op jit(solution)/shard_map/all_to_all | solution.py:54
  65.2 0.8 broadcast_in_dim.18
  66.0 4.1 %all-to-all-start.2 = ((bf16[4,16,4096]{2,1,0:T(8,128)(2,1)}), bf16[4,16,4096]{2,1,0:T(8,128)(2,1)}, u32[]{:S(2)}, u32[]{:S(2)}) async-start(bf16[4,16,4096]{2,1,0:T(8,128)(2,1)} %broadcast_in_dim.18), calls=%async_computation.2 | async-start | bytes 1048576 | tf_op jit(solution)/shard_map/all_to_all | solution.py:62
  70.2 0.5 iota_compare_fusion
  70.7 0.7 bitcast_convert_fusion
  71.4 5.7 %all-to-all-done.2 = bf16[4,16,4096]{2,1,0:T(8,128)(2,1)} async-done(((bf16[4,16,4096]{2,1,0:T(8,128)(2,1)}), bf16[4,16,4096]{2,1,0:T(8,128)(2,1)}, u32[]{:S(2)}, u32[]{:S(2)}) %all-to-all-start.2) | async-done | bytes 524320 | tf_op jit(solution)/shard_map/all_to_all | solution.py:62
  77.2 1.2 %select_reduce_fusion = f32[16,4096]{1,0:T(8,128)S(1)} fusion(bf16[4,16,4096]{2,1,0:T(8,128)(2,1)} %all-to-all-done.2, pred[4]{0:T(512)(128)(4,1)} %iota_compare_fusion), kind=kLoop, calls=%fused_computation.12 | loop fusion | flops 720896 | bytes 786436 | tf_op jit(solution)/shard_map/reduce_sum | solution.py:64
  78.4 6.7 %all_gather.8 = f32[2,16,4096]{2,1,0:T(8,128)} all-gather(f32[1,16,4096]{2,1,0:T(8,128)S(1)} %bitcast_select_fusion), channel_id=1, replica_groups=mesh['x'=4,'core'=2,'seq'=64] {'core'}, dimensions={0}, use_global_device_ids=true | all-gather | bytes 786432 | tf_op jit(solution)/shard_map/all_gather | solution.py:66
  85.1 1.5 %fusion.16 = f32[16]{0:T(128)S(1)} fusion(f32[16,4096]{1,0:T(8,128)S(1)} %select_reduce_fusion, f32[32,2,8,128]{3,2,1,0:T(8,128)} %bitcast_convert_fusion, bf16[16,4096]{1,0:T(8,128)(2,1)} %param.6, bf16[8,16,4096]{2,1,0:T(8,128)(2,1)} %all-gather.2.cloned.1.call-done, s32[]{:T(128)S(6)} %select_n.89, f32[4096]{0:T(1024)S(1)} %bitcast.94, pred[]{:T(512)S(6)} %eq.14, ...), kind=kLoop, calls=%fused_computation.24 | loop fusion | flops 720880 | bytes 1458246 | tf_op jit(solution)/shard_map/reduce_sum | solution.py:71
  87.1 1.8 %fusion.11 = bf16[1,16,4096]{2,1,0:T(8,128)(2,1)} fusion(f32[16,4096]{1,0:T(8,128)S(1)} %select_reduce_fusion, f32[4096]{0:T(1024)S(1)} %bitcast.95, bf16[8,16,4096]{2,1,0:T(8,128)(2,1)} %all-gather.2.cloned.1.call-done, f32[2,16,4096]{2,1,0:T(8,128)} %all_gather.8, pred[]{:T(512)S(6)} %eq.13, bf16[64,8,128]{2,1,0:T(8,128)(2,1)S(1)} %all-to-all-done.1), kind=kLoop, calls=%fused_computation.19 | loop fusion | flops 524288 | bytes 1196033 | tf_op jit(solution)/shard_map/convert_element_type | solution.py:72
  (13 shorter events, 1.0 us)
Async XLA Ops:
  7.2 31.6 %copy-start = (bf16[3,32,128,128]{3,2,1,0:T(8,128)(2,1)S(1)}, bf16[3,32,128,128]{3,2,1,0:T(8,128)(2,1)}, u32[]{:S(2)}) copy-start(bf16[3,32,128,128]{3,2,1,0:T(8,128)(2,1)} %param.9) | copy-start | bytes 9437188
  9.0 29.7 %all-to-all-start = ((bf16[64,16,128]{2,1,0:T(8,128)(2,1)}), bf16[64,16,128]{2,1,0:T(8,128)(2,1)S(1)}, u32[]{:S(2)}, u32[]{:S(2)}) async-start(bf16[64,16,128]{2,1,0:T(8,128)(2,1)} %bitcast.87), calls=%async_computation | async-start | bytes 524288 | tf_op jit(solution)/shard_map/all_to_all | solution.py:50
  26.2 58.9 %all-gather.2.cloned.1.call-start = ((), (), s32[]{:S(2)}) async-start(), calls=%async_computation.3 | async-start | bytes 1179648 | tf_op jit(solution)/shard_map/all_gather | solution.py:46
  39.8 5.1 %copy-start.1 = (bf16[64,16,128]{2,1,0:T(8,128)(2,1)S(1)}, bf16[64,16,128]{2,1,0:T(8,128)(2,1)}, u32[]{:S(2)}) copy-start(bf16[64,16,128]{2,1,0:T(8,128)(2,1)} %add_convert_fusion) | copy-start | bytes 786436
  47.9 17.3 %all-to-all-start.1 = ((bf16[64,8,128]{2,1,0:T(8,128)(2,1)}), bf16[64,8,128]{2,1,0:T(8,128)(2,1)S(1)}, u32[]{:S(2)}, u32[]{:S(2)}) async-start(bf16[64,8,128]{2,1,0:T(8,128)(2,1)} %fusion.6), calls=%async_computation.1 | async-start | bytes 262144 | tf_op jit(solution)/shard_map/all_to_all | solution.py:54
  66.0 11.1 %all-to-all-start.2 = ((bf16[4,16,4096]{2,1,0:T(8,128)(2,1)}), bf16[4,16,4096]{2,1,0:T(8,128)(2,1)}, u32[]{:S(2)}, u32[]{:S(2)}) async-start(bf16[4,16,4096]{2,1,0:T(8,128)(2,1)} %broadcast_in_dim.18), calls=%async_computation.2 | async-start | bytes 1048576 | tf_op jit(solution)/shard_map/all_to_all | solution.py:62
Sparse Core Ops, SparseCore 0:
  29.2 30.3 all-gather.1

commit v2 on v1

v2 whole, which is shorter than its diff:
```python
import functools
import math

import jax
import jax.numpy as jnp
from jax import lax
from jax.experimental import pallas as pl
from jax.experimental.pallas import tpu as pltpu
from jax.sharding import Mesh, PartitionSpec as P

VMEM = pl.BlockSpec(memory_space=pltpu.VMEM)
HBM = pl.BlockSpec(memory_space=pltpu.HBM)


def call(kernel, shapes, *operands, specs=None, scratch=(), limit=32 << 20):
    return pl.pallas_call(
        kernel,
        out_shape=shapes,
        in_specs=[VMEM] * len(operands) if specs is None else specs,
        out_specs=jax.tree.map(lambda _: VMEM, shapes),
        scratch_shapes=scratch,
        compiler_params=pltpu.CompilerParams(vmem_limit_bytes=limit),
    )(*operands)


def own_head(heads):
    return lax.rem(lax.axis_index("near"), heads)


def cut_kernel(
    latent_hbm, modulation_hbm, weights_hbm, sent_ref, own_ref, modulation_ref, weights_ref, *done
):
    size = sent_ref.shape[2]
    heads = weights_hbm.shape[1]
    copies = sent_ref.shape[0] // heads
    fetches = [
        pltpu.make_async_copy(latent_hbm, own_ref, done[0]),
        pltpu.make_async_copy(modulation_hbm, modulation_ref, done[1]),
        pltpu.make_async_copy(weights_hbm.at[:, own_head(heads)], weights_ref, done[2]),
    ]
    for fetch in fetches:
        fetch.start()
    fetches[0].wait()
    for head in range(heads):
        block = own_ref[:, head * size : (head + 1) * size]
        for copy in range(copies):
            sent_ref[copy * heads + head] = block
    fetches[1].wait()
    fetches[2].wait()


def attend_kernel(chunk, heads, tokens_ref, modulation_ref, weights_ref, mixed_ref):
    total_rows, size = tokens_ref.shape
    queries = mixed_ref.shape[0]
    columns = pl.ds(pl.multiple_of(own_head(heads) * size, size), size)
    shift, scale = modulation_ref[0, :, columns], modulation_ref[1, :, columns]

    def modulate(block):
        return (block.astype(jnp.float32) * (1.0 + scale) + shift).astype(jnp.bfloat16)

    def project(block, which):
        product = jnp.dot(block, weights_ref[which], preferred_element_type=jnp.float32)
        return product.astype(jnp.bfloat16)

    every = modulate(tokens_ref[...])
    start = pl.multiple_of(lax.axis_index("far") * queries, queries)
    query = project(modulate(tokens_ref[pl.ds(start, queries), :]), 0)
    key, value = project(every, 1), project(every, 2)
    factor = math.log2(math.e) / math.sqrt(size)
    for start in range(0, queries, chunk):
        scores = lax.dot_general(
            query[start : start + chunk],
            key,
            (((1,), (1,)), ((), ())),
            preferred_element_type=jnp.float32,
        )
        row_max = jnp.max(scores, axis=-1, keepdims=True)
        probs = jnp.exp2(scores * factor - row_max * factor)
        total = jnp.sum(probs, axis=-1, keepdims=True)
        mixed = jnp.dot(probs.astype(jnp.bfloat16), value, preferred_element_type=jnp.float32)
        mixed_ref[start : start + chunk, :] = (mixed / total).astype(jnp.bfloat16)


def spread_kernel(times_ref, modulation_ref, back_ref, own_ref, drift_ref, sent_ref):
    heads, _, size = back_ref.shape
    across = sent_ref.shape[0]
    own_x = lax.axis_index("x")
    time = own_x * lax.axis_size("core") + lax.axis_index("core")
    times = times_ref[...].astype(jnp.float32) / 1000.0
    sigmas = 5.0 * times / (1.0 + 4.0 * times)
    points = lax.broadcasted_iota(jnp.int32, sigmas.shape, 1)
    signed = jnp.where(points == time + 1, sigmas, jnp.where(points == time, -sigmas, 0.0))
    step = jnp.sum(signed, axis=-1, keepdims=True)
    for head in range(heads):
        columns = slice(head * size, (head + 1) * size)
        own = own_ref[:, columns]
        drift = (step * modulation_ref[2, :, columns]) * back_ref[head].astype(jnp.float32)
        drift = drift + jnp.where(time == 0, own.astype(jnp.float32), 0.0)
        drift_ref[:, columns] = drift
        low = drift.astype(jnp.bfloat16)
        for target in range(across):
            sent_ref[target, :, columns] = jnp.where(target > own_x, low, own)


def gather_kernel(own_ref, drift_ref, along_ref, upto_ref, given_ref):
    across, rows, width = along_ref.shape
    own_x, odd = lax.axis_index("x"), lax.axis_index("core") == 1
    later = jnp.minimum(own_x + 1, across - 1)
    for start in range(0, width, 512):
        columns = slice(start, start + 512)
        earlier = jnp.zeros((rows, 512), jnp.float32)
        for source in range(across - 1):
            term = along_ref[source, :, columns].astype(jnp.float32)
            earlier = earlier + jnp.where(source < own_x, term, 0.0)
        upto = earlier + drift_ref[:, columns]
        upto_ref[:, columns] = upto
        given_ref[:rows, columns] = jnp.where(odd, earlier, upto).astype(jnp.bfloat16)
        given_ref[rows:, columns] = jnp.where(odd, own_ref[:, columns], along_ref[later, :, columns])


def finish_kernel(upto_ref, pairs_ref, end_ref, new_ref, error_ref):
    rows, width = upto_ref.shape
    odd = lax.axis_index("core") == 1
    last = jnp.logical_and(odd, lax.axis_index("x") == lax.axis_size("x") - 1)
    squares = jnp.zeros((rows, 128), jnp.float32)
    for start in range(0, width, 512):
        columns = slice(start, start + 512)
        other = jnp.where(odd, pairs_ref[0, :, columns], pairs_ref[1, :, columns])
        updated = upto_ref[:, columns] + other[:rows].astype(jnp.float32)
        new_ref[:, columns] = updated.astype(jnp.bfloat16)
        old = jnp.where(last, end_ref[:, columns], other[rows:])
        change = updated - old.astype(jnp.float32)
        change = change * change
        for part in range(0, 512, 128):
            squares = squares + change[:, part : part + 128]
    error_ref[...] = jnp.sum(squares.T, axis=0, keepdims=True) * (1.0 / width)


def body(latents, end_latent, timesteps, modulation, proj_weight):
    heads, size = proj_weight.shape[1], proj_weight.shape[2]
    rows, width = latents.shape[1:]
    across, group = lax.axis_size("x"), lax.axis_size("far") * lax.axis_size("near")
    copies = group // heads

    def low(*shape):
        return jax.ShapeDtypeStruct(shape, jnp.bfloat16)

    def wide(*shape):
        return jax.ShapeDtypeStruct(shape, jnp.float32)

    sent, own_latent, modulation, weights = call(
        cut_kernel,
        [low(group, rows, size), low(rows, width), wide(3, 1, width), low(3, size, size)],
        *(
            pltpu.with_memory_space_constraint(operand, pltpu.HBM)
            for operand in (latents[0], modulation.transpose(1, 0, 2), proj_weight)
        ),
        specs=[HBM] * 3,
        scratch=[pltpu.SemaphoreType.DMA] * 3,
    )
    tokens = lax.all_to_all(sent, ("far", "near"), 0, 0, tiled=True).reshape(group * rows, size)
    mixed = call(
        functools.partial(attend_kernel, 128, heads),
        low(group * rows // copies, size),
        tokens,
        modulation,
        weights,
    ).reshape(heads, rows, size)
    back = lax.all_to_all(mixed, "near", 0, 0, tiled=True)
    drift, along = call(
        spread_kernel,
        [wide(rows, width), low(across, rows, width)],
        timesteps.reshape(1, -1),
        modulation,
        back,
        own_latent,
    )
    along = lax.all_to_all(along, "x", 0, 0, tiled=True)
    upto, given = call(
        gather_kernel, [wide(rows, width), low(2 * rows, width)], own_latent, drift, along
    )
    pairs = lax.all_gather(given, "core")
    new, error = call(finish_kernel, [low(rows, width), wide(1, rows)], upto, pairs, end_latent)
    return (new[None], error)


def solution(mesh):
    inner = Mesh(
        mesh.devices.reshape(-1, 2, mesh.shape["seq"] // 32, 32), ("x", "core", "far", "near")
    )
    time, seq = ("x", "core"), ("far", "near")
    return jax.shard_map(
        body,
        mesh=inner,
        in_specs=(P(time, seq, None), P(seq, None), P(), P(time, None, None), P()),
        out_specs=(P(time, seq, None), P(time, seq)),
        check_vma=False,
    )
```

time: 96.3 us -> 65.3 us (0.68)
  blocking collectives: 6.66 us -> 60.5 us
  starting transfers between devices: 27.1 us -> 0 us
  waiting for transfers between devices: 25.6 us -> 0 us
  between operations: 15.5 us -> 0.68 us
  other arithmetic: 11.4 us -> 0 us
  matrix products: 6.18 us -> 0 us
  Pallas kernels: 0 us -> 3.89 us
  local copies, waits for them, and re-layouts: 3.36 us -> 0.01 us
    all_to_all x0 -> x3, blocking collectives: none -> 54.1 us  [the longest x1 29.5 us: body(): lax.all_to_all(sent, ('far', 'near'), 0, 0, tiled=True)]
    all_to_all x3 -> x0, starting transfers between devices: 27.1 us -> none  [the longest x1 17.1 us: body(): tokens = lax.all_to_all(sent, 'seq', 0, 0, tiled=True)]
    all_to_all x3 -> x0, waiting for transfers between devices: 24.9 us -> none  [the longest x1 10.8 us: body(): returned = lax.all_to_all(mixed, 'seq', 0, 0, tiled=True)]
    dot_general x3 -> x0, matrix products: 6.18 us -> none  [the longest x1 3.02 us: attend(): jnp.dot(probs.astype(jnp.bfloat16), value, preferred_element_type=jnp.flo...]
    reduce_sum x3 -> x0, other arithmetic: 4.77 us -> none  [the longest x1 2.08 us: attend(): total = jnp.sum(probs, axis=-1, keepdims=True)]
    pallas_call x0 -> x5, Pallas kernels: none -> 3.89 us  [call(): pl.pallas_call(kernel, out_shape=shapes, in_specs=[VMEM] * len(operands)...]
    convert_element_type x4 -> x0, other arithmetic: 3.33 us -> none  [the longest x1 1.81 us: body(): return (updated.astype(jnp.bfloat16)[None], error[None])]
    broadcast_in_dim x2 -> x0, local copies, waits for them, and re-layouts: 1.55 us -> none  [the longest x1 0.83 us: body(): jnp.broadcast_to(drift.astype(jnp.bfloat16)[None], (across, rows, width))]
  transfers between devices with their start and end apart: 4 -> 0, of which waited for: 3 -> 0; matrix products, arithmetic and copies ran while one was open for 16% -> 0% of each run, Pallas kernels for 0% -> 0%
where the time goes in v2:
time: 65.3 us; the launch traced here: 65 us
  blocking collectives  60.5 us (93%)
  Pallas kernels  3.89 us (6%)
  between operations  0.68 us (1%)
    all_to_all x1, blocking collectives, body(): lax.all_to_all(sent, ('far', 'near'), 0, 0, tiled=True)  29.5 us
    all_to_all x1, blocking collectives, body(): back = lax.all_to_all(mixed, 'near', 0, 0, tiled=True)  13.9 us
    all_to_all x1, blocking collectives, body(): along = lax.all_to_all(along, 'x', 0, 0, tiled=True)  10.7 us
    all_gather x1, blocking collectives, body(): pairs = lax.all_gather(given, 'core')  6.3 us
    pallas_call x5, Pallas kernels, call(): pl.pallas_call(kernel, out_shape=shapes, in_specs=[VMEM] * len(operands)...  3.89 us

profile of v2, /device:TPU:1, one launch (start us, length us, event | category | flops | bytes accessed | tf_op | source)
XLA Modules:
  0.0 65.0 jit_solution(6386046032513558277)
XLA Ops:
  0.6 0.0 copy-start.1
  0.6 0.0 copy-start
  0.7 1.0 %shard_map.68 = (bf16[64,16,128]{2,1,0:T(8,128)(2,1)S(1)}, bf16[16,4096]{1,0:T(8,128)(2,1)S(1)}, f32[3,1,4096]{2,1,0:T(1,128)S(1)}, bf16[3,128,128]{2,1,0:T(8,128)(2,1)S(1)}) custom-call(bf16[16,4096]{1,0:T(8,128)(2,1)} %bitcast.11, f32[3,1,4096]{2,1,0:T(1,128)} %bitcast.12, bf16[3,32,128,128]{3,2,1,0:T(8,128)(2,1)} %weights_hbm.1), custom_call_target="tpu_custom_call" | custom-call | tf_op jit(solution)/shard_map/pallas_call | solution.py:16
  1.7 29.5 %all_to_all.15 = bf16[64,16,128]{2,1,0:T(8,128)(2,1)S(1)} all-to-all(bf16[64,16,128]{2,1,0:T(8,128)(2,1)S(1)} %get-tuple-element.14), channel_id=1, replica_groups=mesh['x'=4,'core'=2,'far'=2,'near'=32] {'far','near'}, dimensions={0} | all-to-all | bytes 524288 | tf_op jit(solution)/shard_map/all_to_all | solution.py:161
  31.2 1.8 %shard_map.69 = bf16[512,128]{1,0:T(8,128)(2,1)S(1)} custom-call(bf16[1024,128]{1,0:T(8,128)(2,1)S(1)} %bitcast.8, f32[3,1,4096]{2,1,0:T(1,128)S(1)} %get-tuple-element.13.modulation_ref, bf16[3,128,128]{2,1,0:T(8,128)(2,1)S(1)} %get-tuple-element.15.weights_ref), custom_call_target="tpu_custom_call" | custom-call | tf_op jit(solution)/shard_map/pallas_call | solution.py:16
  33.0 13.9 %all_to_all.16.back_ref = bf16[32,16,128]{2,1,0:T(8,128)(2,1)S(1)} all-to-all(bf16[32,16,128]{2,1,0:T(8,128)(2,1)S(1)} %bitcast.9), channel_id=1, replica_groups=mesh['x'=4,'core'=2,'far'=2,'near'=32] {'near'}, dimensions={0} | all-to-all | bytes 262144 | tf_op jit(solution)/shard_map/all_to_all | solution.py:169
  46.9 0.0 copy-done.1
  46.9 0.2 shard_map.70
  47.1 10.7 %all_to_all.17.along_ref = bf16[4,16,4096]{2,1,0:T(8,128)(2,1)S(1)} all-to-all(bf16[4,16,4096]{2,1,0:T(8,128)(2,1)S(1)} %get-tuple-element.17), channel_id=1, replica_groups=mesh['x'=4,'core'=2,'far'=2,'near'=32] {'x'}, dimensions={0} | all-to-all | bytes 1048576 | tf_op jit(solution)/shard_map/all_to_all | solution.py:178
  57.9 0.1 shard_map.71
  58.0 6.3 %all-gather = bf16[64,4096]{1,0:T(8,128)(2,1)S(1)} all-gather(bf16[32,4096]{1,0:T(8,128)(2,1)S(1)} %get-tuple-element.19), channel_id=2, replica_groups=mesh['x'=4,'core'=2,'far'=2,'near'=32] {'core'}, dimensions={0}, use_global_device_ids=true | all-gather | bytes 786432 | tf_op jit(solution)/shard_map/all_gather | solution.py:182
  64.3 0.0 copy-done
  64.3 0.7 %shard_map.72 = (bf16[16,4096]{1,0:T(8,128)(2,1)}, f32[1,16]{1,0:T(1,128)}) custom-call(f32[16,4096]{1,0:T(8,128)S(1)} %get-tuple-element.18.upto_ref, bf16[2,32,4096]{2,1,0:T(8,128)(2,1)S(1)} %bitcast.7, bf16[16,4096]{1,0:T(8,128)(2,1)S(1)} %copy-done), custom_call_target="tpu_custom_call" | custom-call | tf_op jit(solution)/shard_map/pallas_call | solution.py:16
Async XLA Ops:
  0.6 46.3 %copy-start.1 = (s32[9]{0:T(128)S(1)}, s32[9]{0:T(128)}, u32[]{:S(2)}) copy-start(s32[9]{0:T(128)} %param.7) | copy-start | bytes 112
  0.6 63.7 %copy-start = (bf16[16,4096]{1,0:T(8,128)(2,1)S(1)}, bf16[16,4096]{1,0:T(8,128)(2,1)}, u32[]{:S(2)}) copy-start(bf16[16,4096]{1,0:T(8,128)(2,1)} %end_ref.1) | copy-start | bytes 393220

commit v3 on v2

v3 whole, which is shorter than its diff:
```python
import functools
import math

import jax
import jax.numpy as jnp
from jax import lax
from jax.experimental import pallas as pl
from jax.experimental.pallas import tpu as pltpu
from jax.sharding import Mesh, PartitionSpec as P

VMEM = pl.BlockSpec(memory_space=pltpu.VMEM)
HBM = pl.BlockSpec(memory_space=pltpu.HBM)


def call(kernel, shapes, *operands, specs=None, scratch=()):
    return pl.pallas_call(
        kernel,
        out_shape=shapes,
        in_specs=[VMEM] * len(operands) if specs is None else specs,
        out_specs=jax.tree.map(lambda _: VMEM, shapes),
        scratch_shapes=scratch,
        compiler_params=pltpu.CompilerParams(vmem_limit_bytes=32 << 20),
    )(*operands)


BITS = ("y2", "y1", "y0", "z2", "z1", "z0")
ORDER = ('y0', 'y1', 'y2', 'z2', 'z1', 'z0')
FAR = "z2"
NEAR = tuple(axis for axis in ORDER if axis != FAR)
ACROSS = ("x1", "x0")
AFTER = 1 << (len(ORDER) - 1 - ORDER.index(FAR))


def step_size(times_ref, time):
    times = times_ref[...].astype(jnp.float32) / 1000.0
    sigmas = 5.0 * times / (1.0 + 4.0 * times)
    points = lax.broadcasted_iota(jnp.int32, sigmas.shape, 1)
    signed = jnp.where(points == time + 1, sigmas, jnp.where(points == time, -sigmas, 0.0))
    return jnp.sum(signed, axis=-1, keepdims=True)


def own_time():
    return lax.axis_index(ACROSS) * lax.axis_size("core") + lax.axis_index("core")


def cut_kernel(
    latent_hbm, weights_hbm, modulation_hbm, times_hbm, end_hbm,
    sent_ref, own_ref, weights_ref, modulation_ref, times_ref, end_ref,
    *done,
):
    before, copies, after, _, size = sent_ref.shape
    fetches = [
        pltpu.make_async_copy(source, target, semaphore)
        for source, target, semaphore in (
            (latent_hbm, own_ref, done[0]),
            (weights_hbm.at[:, lax.axis_index(NEAR)], weights_ref, done[1]),
            (modulation_hbm, modulation_ref, done[2]),
            (times_hbm, times_ref, done[3]),
            (end_hbm, end_ref, done[4]),
        )
    ]
    for fetch in fetches:
        fetch.start()
    fetches[0].wait()
    for head in range(before * after):
        block = own_ref[:, head * size : (head + 1) * size]
        for copy in range(copies):
            sent_ref[head // after, copy, head % after] = block
    for fetch in fetches[1:]:
        fetch.wait()


def attend_kernel(chunk, tokens_ref, times_ref, modulation_ref, weights_ref, sent_ref):
    across, queries, size = sent_ref.shape
    columns = pl.ds(pl.multiple_of(lax.axis_index(NEAR) * size, size), size)
    own_x, time = lax.axis_index(ACROSS), own_time()
    shift, scale = modulation_ref[0, :, columns], modulation_ref[1, :, columns]
    rate = step_size(times_ref, time) * modulation_ref[2, :, columns]

    def modulate(block):
        return (block.astype(jnp.float32) * (1.0 + scale) + shift).astype(jnp.bfloat16)

    def project(block, which):
        product = jnp.dot(block, weights_ref[which], preferred_element_type=jnp.float32)
        return product.astype(jnp.bfloat16)

    every = modulate(tokens_ref[...].reshape(2 * queries, size))
    latent = tokens_ref[:, lax.axis_index(FAR)].reshape(queries, size)
    query, key, value = project(modulate(latent), 0), project(every, 1), project(every, 2)
    factor = math.log2(math.e) / math.sqrt(size)

    def score(start):
        block = query[start : start + chunk]
        return lax.dot_general(
            block, key, (((1,), (1,)), ((), ())), preferred_element_type=jnp.float32
        )

    following = score(0)
    for start in range(0, queries, chunk):
        scores = following
        if start + chunk < queries:
            following = score(start + chunk)
        row_max = jnp.max(scores, axis=-1, keepdims=True)
        probs = jnp.exp2(scores * factor - row_max * factor)
        total = jnp.sum(probs, axis=-1, keepdims=True)
        mixed = jnp.dot(probs.astype(jnp.bfloat16), value, preferred_element_type=jnp.float32)
        mixed = (mixed / total).astype(jnp.bfloat16)
        old = latent[start : start + chunk]
        drift = rate * mixed.astype(jnp.float32)
        drift = drift + jnp.where(time == 0, old.astype(jnp.float32), 0.0)
        drift = drift.astype(jnp.bfloat16)
        for target in range(across):
            earlier = jnp.where(target < own_x, old, mixed)
            sent_ref[target, start : start + chunk, :] = jnp.where(target > own_x, drift, earlier)


def gather_kernel(times_ref, modulation_ref, own_ref, along_ref, upto_ref, given_ref):
    across, heads, rows, size = along_ref.shape
    own_x, odd, time = lax.axis_index(ACROSS), lax.axis_index("core") == 1, own_time()
    later = jnp.minimum(own_x + 1, across - 1)
    step = step_size(times_ref, time)
    for head in range(heads):
        columns = slice(head * size, (head + 1) * size)
        own = own_ref[:, columns]
        earlier = jnp.zeros((rows, size), jnp.float32)
        for source in range(across - 1):
            term = along_ref[source, head].astype(jnp.float32)
            earlier = earlier + jnp.where(source < own_x, term, 0.0)
        drift = (step * modulation_ref[2, :, columns]) * along_ref[own_x, head].astype(jnp.float32)
        first = jnp.where(time == 0, own.astype(jnp.float32), 0.0)
        upto = earlier + (drift + first)
        upto_ref[:, columns] = upto
        given_ref[:rows, columns] = jnp.where(odd, earlier, upto).astype(jnp.bfloat16)
        given_ref[rows:, columns] = jnp.where(odd, own, along_ref[later, head])


def finish_kernel(upto_ref, pairs_ref, end_ref, new_ref, error_ref):
    rows, width = upto_ref.shape
    odd = lax.axis_index("core") == 1
    last = jnp.logical_and(odd, lax.axis_index(ACROSS) == lax.axis_size(ACROSS) - 1)
    squares = jnp.zeros((rows, 128), jnp.float32)
    for start in range(0, width, 512):
        columns = slice(start, start + 512)
        other = jnp.where(odd, pairs_ref[0, :, columns], pairs_ref[1, :, columns])
        updated = upto_ref[:, columns] + other[:rows].astype(jnp.float32)
        new_ref[:, columns] = updated.astype(jnp.bfloat16)
        old = jnp.where(last, end_ref[:, columns], other[rows:])
        change = updated - old.astype(jnp.float32)
        change = change * change
        for part in range(0, 512, 128):
            squares = squares + change[:, part : part + 128]
    error_ref[...] = jnp.sum(squares.T, axis=0, keepdims=True) * (1.0 / width)


def body(latents, end_latent, timesteps, modulation, proj_weight):
    heads, size = proj_weight.shape[1], proj_weight.shape[2]
    rows, width = latents.shape[1:]
    across, group = lax.axis_size(ACROSS), lax.axis_size(ORDER)
    copies = group // heads

    def low(*shape):
        return jax.ShapeDtypeStruct(shape, jnp.bfloat16)

    def wide(*shape):
        return jax.ShapeDtypeStruct(shape, jnp.float32)

    inputs = (
        latents[0],
        proj_weight,
        modulation.transpose(1, 0, 2),
        timesteps.reshape(1, -1),
        end_latent,
    )
    sent, own_latent, weights, modulation, timesteps, end_latent = call(
        cut_kernel,
        [
            low(heads // AFTER, copies, AFTER, rows, size),
            low(rows, width),
            low(3, size, size),
            wide(3, 1, width),
            jax.ShapeDtypeStruct((1, timesteps.shape[0]), jnp.int32),
            low(rows, width),
        ],
        *(pltpu.with_memory_space_constraint(operand, pltpu.HBM) for operand in inputs),
        specs=[HBM] * len(inputs),
        scratch=[pltpu.SemaphoreType.DMA] * len(inputs),
    )
    tokens = lax.all_to_all(sent.reshape(group, rows, size), ORDER, 0, 0, tiled=True)
    sent = call(
        functools.partial(attend_kernel, 256),
        low(across, heads * rows, size),
        tokens.reshape(heads // AFTER, copies, AFTER * rows, size),
        timesteps,
        modulation,
        weights,
    )
    along = lax.all_to_all(
        sent.reshape(across * heads, rows, size), ACROSS + NEAR, 0, 0, tiled=True
    )
    upto, given = call(
        gather_kernel,
        [wide(rows, width), low(2 * rows, width)],
        timesteps,
        modulation,
        own_latent,
        along.reshape(across, heads, rows, size),
    )
    pairs = lax.all_gather(given, "core")
    new, error = call(finish_kernel, [low(rows, width), wide(1, rows)], upto, pairs, end_latent)
    return (new[None], error)


def solution(mesh):
    names = ACROSS + ("core",) + BITS
    inner = Mesh(mesh.devices.reshape((2,) * len(names)), names)
    time = ACROSS + ("core",)
    return jax.shard_map(
        body,
        mesh=inner,
        in_specs=(P(time, BITS, None), P(BITS, None), P(), P(time, None, None), P()),
        out_specs=(P(time, BITS, None), P(time, BITS)),
        check_vma=False,
    )
```

time: 65.3 us -> 64 us (0.980)
    pallas_call x5 -> x4, Pallas kernels: 3.89 us -> 3.31 us  [call(): pl.pallas_call(kernel, out_shape=shapes, in_specs=[VMEM] * len(operands)...]
    all_to_all x3 -> x2, blocking collectives: 54.1 us -> 54 us  [the longest x1 28.8 us: body(): lax.all_to_all(sent.reshape(group, rows, size), ORDER, 0, 0, tiled=True)]
where the time goes in v3:
time: 64 us; the launch traced here: 63.9 us
  blocking collectives  59.9 us (94%)
  Pallas kernels  3.31 us (5%)
  between operations  0.65 us (1%)
    all_to_all x1, blocking collectives, body(): lax.all_to_all(sent.reshape(group, rows, size), ORDER, 0, 0, tiled=True)  28.8 us
    all_to_all x1, blocking collectives, body(): lax.all_to_all(sent.reshape(across * heads, rows, size), ACROSS + NEAR, 0...  25.2 us
    all_gather x1, blocking collectives, body(): pairs = lax.all_gather(given, 'core')  5.87 us
    pallas_call x4, Pallas kernels, call(): pl.pallas_call(kernel, out_shape=shapes, in_specs=[VMEM] * len(operands)...  3.31 us

profile of v3, /device:TPU:1, one launch (start us, length us, event | category | flops | bytes accessed | tf_op | source)
XLA Modules:
  0.0 63.9 jit_solution(8500737101547074952)
XLA Ops:
  0.6 1.1 %shard_map.68 = (bf16[8,2,4,16,128]{4,3,2,1,0:T(8,128)(2,1)S(1)}, bf16[16,4096]{1,0:T(8,128)(2,1)S(1)}, bf16[3,128,128]{2,1,0:T(8,128)(2,1)S(1)}, f32[3,1,4096]{...) custom-call(bf16[16,4096]{1,0:T(8,128)(2,1)} %bitcast.14, bf16[3,32,128,128]{3,2,1,0:T(8,128)(2,1)} %weights_hbm.1, ...), custom_call_target="tpu_custom_call" | custom-call | tf_op jit(solution)/shard_map/pallas_call | solution.py:16
  1.7 28.8 %all_to_all.10 = bf16[64,16,128]{2,1,0:T(8,128)(2,1)S(1)} all-to-all(bf16[64,16,128]{2,1,0:T(8,128)(2,1)S(1)} %bitcast.13), channel_id=1, replica_groups=mesh['x1'=2,'x0'=2,'core'=2,'y2'=2,'y1'=2,'y0'=2,'z2'=2,'z1'=2,'z0'=2] {..., dimensions={0} | all-to-all | bytes 524288 | tf_op jit(solution)/shard_map/all_to_all | solution.py:188
  30.6 1.3 %shard_map.69 = bf16[4,512,128]{2,1,0:T(8,128)(2,1)S(1)} custom-call(bf16[8,2,64,128]{3,2,1,0:T(8,128)(2,1)S(1)} %bitcast.12, s32[1,9]{1,0:T(1,128)S(1)} %get-tuple-element.12.times_ref, f32[3,1,4096]{2,1,0:T(1,128)S(1)} %get-tuple-element.13.modulation_ref, bf16[3,128,128]{2,1,0:T(8,128)(2,1)S(1)} %get-tuple-element.16.weights_ref), custom_call_target="tpu_custom_call" | custom-call | tf_op jit(solution)/shard_map/pallas_call | solution.py:16
  31.9 25.2 %all_to_all.11 = bf16[128,16,128]{2,1,0:T(8,128)(2,1)S(1)} all-to-all(bf16[128,16,128]{2,1,0:T(8,128)(2,1)S(1)} %bitcast.11), channel_id=1, replica_groups=mesh['x1'=2,'x0'=2,'core'=2,'y2'=2,'y1'=2,'y0'=2,'z2'=2,'z1'=2,'z0'=2] {..., dimensions={0} | all-to-all | bytes 1048576 | tf_op jit(solution)/shard_map/all_to_all | solution.py:197
  57.1 0.2 shard_map.70
  57.2 5.9 %all-gather = bf16[64,4096]{1,0:T(8,128)(2,1)S(1)} all-gather(bf16[32,4096]{1,0:T(8,128)(2,1)S(1)} %get-tuple-element.18), channel_id=2, replica_groups=mesh['x1'=2,'x0'=2,'core'=2,'y2'=2,'y1'=2,'y0'=2,'z2'=2,'z1'=2,'z0'=2] {..., dimensions={0}, use_global_device_ids=true | all-gather | bytes 786432 | tf_op jit(solution)/shard_map/all_gather | solution.py:208
  63.1 0.7 %shard_map.71 = (bf16[16,4096]{1,0:T(8,128)(2,1)}, f32[1,16]{1,0:T(1,128)}) custom-call(f32[16,4096]{1,0:T(8,128)S(1)} %get-tuple-element.17.upto_ref, bf16[2,32,4096]{2,1,0:T(8,128)(2,1)S(1)} %bitcast.9, bf16[16,4096]{1,0:T(8,128)(2,1)S(1)} %get-tuple-element.19.end_ref), custom_call_target="tpu_custom_call" | custom-call | tf_op jit(solution)/shard_map/pallas_call | solution.py:16

commit v4 on v3

--- a/solution.py
+++ b/solution.py
@@ -71,7 +71,8 @@
 
 
 def attend_kernel(chunk, tokens_ref, times_ref, modulation_ref, weights_ref, sent_ref):
-    across, queries, size = sent_ref.shape
+    heads, across, rows, size = sent_ref.shape
+    queries = heads * rows
     columns = pl.ds(pl.multiple_of(lax.axis_index(NEAR) * size, size), size)
     own_x, time = lax.axis_index(ACROSS), own_time()
     shift, scale = modulation_ref[0, :, columns], modulation_ref[1, :, columns]
@@ -101,7 +102,7 @@
         if start + chunk < queries:
             following = score(start + chunk)
         row_max = jnp.max(scores, axis=-1, keepdims=True)
-        probs = jnp.exp2(scores * factor - row_max * factor)
+        probs = jnp.exp2((scores - row_max) * factor)
         total = jnp.sum(probs, axis=-1, keepdims=True)
         mixed = jnp.dot(probs.astype(jnp.bfloat16), value, preferred_element_type=jnp.float32)
         mixed = (mixed / total).astype(jnp.bfloat16)
@@ -111,11 +112,12 @@
         drift = drift.astype(jnp.bfloat16)
         for target in range(across):
             earlier = jnp.where(target < own_x, old, mixed)
-            sent_ref[target, start : start + chunk, :] = jnp.where(target > own_x, drift, earlier)
+            block = jnp.where(target > own_x, drift, earlier)
+            sent_ref[start // rows : (start + chunk) // rows, target] = block.reshape(chunk // rows, rows, size)
 
 
 def gather_kernel(times_ref, modulation_ref, own_ref, along_ref, upto_ref, given_ref):
-    across, heads, rows, size = along_ref.shape
+    heads, across, rows, size = along_ref.shape
     own_x, odd, time = lax.axis_index(ACROSS), lax.axis_index("core") == 1, own_time()
     later = jnp.minimum(own_x + 1, across - 1)
     step = step_size(times_ref, time)
@@ -124,14 +126,14 @@
         own = own_ref[:, columns]
         earlier = jnp.zeros((rows, size), jnp.float32)
         for source in range(across - 1):
-            term = along_ref[source, head].astype(jnp.float32)
+            term = along_ref[head, source].astype(jnp.float32)
             earlier = earlier + jnp.where(source < own_x, term, 0.0)
-        drift = (step * modulation_ref[2, :, columns]) * along_ref[own_x, head].astype(jnp.float32)
+        drift = (step * modulation_ref[2, :, columns]) * along_ref[head, own_x].astype(jnp.float32)
         first = jnp.where(time == 0, own.astype(jnp.float32), 0.0)
         upto = earlier + (drift + first)
         upto_ref[:, columns] = upto
         given_ref[:rows, columns] = jnp.where(odd, earlier, upto).astype(jnp.bfloat16)
-        given_ref[rows:, columns] = jnp.where(odd, own, along_ref[later, head])
+        given_ref[rows:, columns] = jnp.where(odd, own, along_ref[head, later])
 
 
 def finish_kernel(upto_ref, pairs_ref, end_ref, new_ref, error_ref):
@@ -188,14 +190,14 @@
     tokens = lax.all_to_all(sent.reshape(group, rows, size), ORDER, 0, 0, tiled=True)
     sent = call(
         functools.partial(attend_kernel, 256),
-        low(across, heads * rows, size),
+        low(heads, across, rows, size),
         tokens.reshape(heads // AFTER, copies, AFTER * rows, size),
         timesteps,
         modulation,
         weights,
     )
     along = lax.all_to_all(
-        sent.reshape(across * heads, rows, size), ACROSS + NEAR, 0, 0, tiled=True
+        sent.reshape(across * heads, rows, size), NEAR + ACROSS, 0, 0, tiled=True
     )
     upto, given = call(
         gather_kernel,
@@ -203,7 +205,7 @@
         timesteps,
         modulation,
         own_latent,
-        along.reshape(across, heads, rows, size),
+        along.reshape(heads, across, rows, size),
     )
     pairs = lax.all_gather(given, "core")
     new, error = call(finish_kernel, [low(rows, width), wide(1, rows)], upto, pairs, end_latent)

time: 64 us -> 63.3 us (0.989)
  blocking collectives: 59.9 us -> 59.2 us
    all_to_all x1, blocking collectives: 25.2 us -> 24.2 us  [body(): lax.all_to_all(sent.reshape(across * heads, rows, size), NEAR + ACROSS, 0...]
where the time goes in v4:
time: 63.3 us; the launch traced here: 63.1 us
  blocking collectives  59.2 us (94%)
  Pallas kernels  3.25 us (5%)
  between operations  0.65 us (1%)
    all_to_all x1, blocking collectives, body(): lax.all_to_all(sent.reshape(group, rows, size), ORDER, 0, 0, tiled=True)  28.8 us
    all_to_all x1, blocking collectives, body(): lax.all_to_all(sent.reshape(across * heads, rows, size), NEAR + ACROSS, 0...  24.2 us
    all_gather x1, blocking collectives, body(): pairs = lax.all_gather(given, 'core')  6.12 us
    pallas_call x4, Pallas kernels, call(): pl.pallas_call(kernel, out_shape=shapes, in_specs=[VMEM] * len(operands)...  3.25 us

profile of v4, /device:TPU:1, one launch (start us, length us, event | category | flops | bytes accessed | tf_op | source)
XLA Modules:
  0.0 63.1 jit_solution(3237968711178125840)
XLA Ops:
  0.6 1.1 %shard_map.68 = (bf16[8,2,4,16,128]{4,3,2,1,0:T(8,128)(2,1)S(1)}, bf16[16,4096]{1,0:T(8,128)(2,1)S(1)}, bf16[3,128,128]{2,1,0:T(8,128)(2,1)S(1)}, f32[3,1,4096]{...) custom-call(bf16[16,4096]{1,0:T(8,128)(2,1)} %bitcast.14, bf16[3,32,128,128]{3,2,1,0:T(8,128)(2,1)} %weights_hbm.1, ...), custom_call_target="tpu_custom_call" | custom-call | tf_op jit(solution)/shard_map/pallas_call | solution.py:16
  1.7 28.8 %all_to_all.10 = bf16[64,16,128]{2,1,0:T(8,128)(2,1)S(1)} all-to-all(bf16[64,16,128]{2,1,0:T(8,128)(2,1)S(1)} %bitcast.13), channel_id=1, replica_groups=mesh['x1'=2,'x0'=2,'core'=2,'y2'=2,'y1'=2,'y0'=2,'z2'=2,'z1'=2,'z0'=2] {..., dimensions={0} | all-to-all | bytes 524288 | tf_op jit(solution)/shard_map/all_to_all | solution.py:190
  30.6 1.2 %shard_map.69 = bf16[32,4,16,128]{3,2,1,0:T(8,128)(2,1)S(1)} custom-call(bf16[8,2,64,128]{3,2,1,0:T(8,128)(2,1)S(1)} %bitcast.12, s32[1,9]{1,0:T(1,128)S(1)} %get-tuple-element.12.times_ref, f32[3,1,4096]{2,1,0:T(1,128)S(1)} %get-tuple-element.13.modulation_ref, bf16[3,128,128]{2,1,0:T(8,128)(2,1)S(1)} %get-tuple-element.16.weights_ref), custom_call_target="tpu_custom_call" | custom-call | tf_op jit(solution)/shard_map/pallas_call | solution.py:16
  31.8 24.2 %all_to_all.11 = bf16[128,16,128]{2,1,0:T(8,128)(2,1)S(1)} all-to-all(bf16[128,16,128]{2,1,0:T(8,128)(2,1)S(1)} %bitcast.11), channel_id=1, replica_groups=mesh['x1'=2,'x0'=2,'core'=2,'y2'=2,'y1'=2,'y0'=2,'z2'=2,'z1'=2,'z0'=2] {..., dimensions={0} | all-to-all | bytes 1048576 | tf_op jit(solution)/shard_map/all_to_all | solution.py:199
  56.0 0.2 shard_map.70
  56.2 6.1 %all-gather = bf16[64,4096]{1,0:T(8,128)(2,1)S(1)} all-gather(bf16[32,4096]{1,0:T(8,128)(2,1)S(1)} %get-tuple-element.18), channel_id=2, replica_groups=mesh['x1'=2,'x0'=2,'core'=2,'y2'=2,'y1'=2,'y0'=2,'z2'=2,'z1'=2,'z0'=2] {..., dimensions={0}, use_global_device_ids=true | all-gather | bytes 786432 | tf_op jit(solution)/shard_map/all_gather | solution.py:210
  62.4 0.7 %shard_map.71 = (bf16[16,4096]{1,0:T(8,128)(2,1)}, f32[1,16]{1,0:T(1,128)}) custom-call(f32[16,4096]{1,0:T(8,128)S(1)} %get-tuple-element.17.upto_ref, bf16[2,32,4096]{2,1,0:T(8,128)(2,1)S(1)} %bitcast.9, bf16[16,4096]{1,0:T(8,128)(2,1)S(1)} %get-tuple-element.19.end_ref), custom_call_target="tpu_custom_call" | custom-call | tf_op jit(solution)/shard_map/pallas_call | solution.py:16

commit v5 on v4

--- a/solution.py
+++ b/solution.py
@@ -24,7 +24,7 @@
 
 
 BITS = ("y2", "y1", "y0", "z2", "z1", "z0")
-ORDER = ('y0', 'y1', 'y2', 'z2', 'z1', 'z0')
+ORDER = ("z2", "y0", "y2", "y1", "z1", "z0")
 FAR = "z2"
 NEAR = tuple(axis for axis in ORDER if axis != FAR)
 ACROSS = ("x1", "x0")

time: 63.3 us -> 63 us (level)
  no operation moved by 1% of the time
where the time goes in v5:
time: 63 us; the launch traced here: 62.8 us
  blocking collectives  58.9 us (93%)
  Pallas kernels  3.26 us (5%)
  between operations  0.65 us (1%)
    all_to_all x1, blocking collectives, body(): lax.all_to_all(sent.reshape(group, rows, size), ORDER, 0, 0, tiled=True)  28.8 us
    all_to_all x1, blocking collectives, body(): lax.all_to_all(sent.reshape(across * heads, rows, size), NEAR + ACROSS, 0...  24.1 us
    all_gather x1, blocking collectives, body(): pairs = lax.all_gather(given, 'core')  5.96 us
    pallas_call x4, Pallas kernels, call(): pl.pallas_call(kernel, out_shape=shapes, in_specs=[VMEM] * len(operands)...  3.26 us

profile of v5, /device:TPU:1, one launch (start us, length us, event | category | flops | bytes accessed | tf_op | source)
XLA Modules:
  0.0 62.8 jit_solution(10437139942235840937)
XLA Ops:
  0.6 1.1 %shard_map.68 = (bf16[1,2,32,16,128]{4,3,2,1,0:T(8,128)(2,1)S(1)}, bf16[16,4096]{1,0:T(8,128)(2,1)S(1)}, bf16[3,128,128]{2,1,0:T(8,128)(2,1)S(1)}, f32[3,1,4096]...) custom-call(bf16[16,4096]{1,0:T(8,128)(2,1)} %bitcast.14, bf16[3,32,128,128]{3,2,1,0:T(8,128)(2,1)} %weights_hbm.1, ...), custom_call_target="tpu_custom_call" | custom-call | tf_op jit(solution)/shard_map/pallas_call | solution.py:16
  1.7 28.8 %all_to_all.10 = bf16[64,16,128]{2,1,0:T(8,128)(2,1)S(1)} all-to-all(bf16[64,16,128]{2,1,0:T(8,128)(2,1)S(1)} %bitcast.13), channel_id=1, replica_groups=mesh['x1'=2,'x0'=2,'core'=2,'y2'=2,'y1'=2,'y0'=2,'z2'=2,'z1'=2,'z0'=2] {..., dimensions={0} | all-to-all | bytes 524288 | tf_op jit(solution)/shard_map/all_to_all | solution.py:190
  30.6 1.2 %shard_map.69 = bf16[32,4,16,128]{3,2,1,0:T(8,128)(2,1)S(1)} custom-call(bf16[1,2,512,128]{3,2,1,0:T(8,128)(2,1)S(1)} %bitcast.12, s32[1,9]{1,0:T(1,128)S(1)} %get-tuple-element.12.times_ref, f32[3,1,4096]{2,1,0:T(1,128)S(1)} %get-tuple-element.13.modulation_ref, bf16[3,128,128]{2,1,0:T(8,128)(2,1)S(1)} %get-tuple-element.16.weights_ref), custom_call_target="tpu_custom_call" | custom-call | tf_op jit(solution)/shard_map/pallas_call | solution.py:16
  31.8 24.1 %all_to_all.11 = bf16[128,16,128]{2,1,0:T(8,128)(2,1)S(1)} all-to-all(bf16[128,16,128]{2,1,0:T(8,128)(2,1)S(1)} %bitcast.11), channel_id=1, replica_groups=mesh['x1'=2,'x0'=2,'core'=2,'y2'=2,'y1'=2,'y0'=2,'z2'=2,'z1'=2,'z0'=2] {..., dimensions={0} | all-to-all | bytes 1048576 | tf_op jit(solution)/shard_map/all_to_all | solution.py:199
  55.9 0.2 shard_map.70
  56.1 6.0 %all-gather = bf16[64,4096]{1,0:T(8,128)(2,1)S(1)} all-gather(bf16[32,4096]{1,0:T(8,128)(2,1)S(1)} %get-tuple-element.18), channel_id=2, replica_groups=mesh['x1'=2,'x0'=2,'core'=2,'y2'=2,'y1'=2,'y0'=2,'z2'=2,'z1'=2,'z0'=2] {..., dimensions={0}, use_global_device_ids=true | all-gather | bytes 786432 | tf_op jit(solution)/shard_map/all_gather | solution.py:210
  62.0 0.7 %shard_map.71 = (bf16[16,4096]{1,0:T(8,128)(2,1)}, f32[1,16]{1,0:T(1,128)}) custom-call(f32[16,4096]{1,0:T(8,128)S(1)} %get-tuple-element.17.upto_ref, bf16[2,32,4096]{2,1,0:T(8,128)(2,1)S(1)} %bitcast.9, bf16[16,4096]{1,0:T(8,128)(2,1)S(1)} %get-tuple-element.19.end_ref), custom_call_target="tpu_custom_call" | custom-call | tf_op jit(solution)/shard_map/pallas_call | solution.py:16

commit v6 on v5

--- a/solution.py
+++ b/solution.py
@@ -71,8 +71,9 @@
 
 
 def attend_kernel(chunk, tokens_ref, times_ref, modulation_ref, weights_ref, sent_ref):
-    heads, across, rows, size = sent_ref.shape
-    queries = heads * rows
+    outer, across, inner, rows, size = sent_ref.shape
+    queries = outer * inner * rows
+    step = inner * rows
     columns = pl.ds(pl.multiple_of(lax.axis_index(NEAR) * size, size), size)
     own_x, time = lax.axis_index(ACROSS), own_time()
     shift, scale = modulation_ref[0, :, columns], modulation_ref[1, :, columns]
@@ -113,11 +114,14 @@
         for target in range(across):
             earlier = jnp.where(target < own_x, old, mixed)
             block = jnp.where(target > own_x, drift, earlier)
-            sent_ref[start // rows : (start + chunk) // rows, target] = block.reshape(chunk // rows, rows, size)
+            sent_ref[start // step : (start + chunk) // step, target] = block.reshape(
+                chunk // step, inner, rows, size
+            )
 
 
 def gather_kernel(times_ref, modulation_ref, own_ref, along_ref, upto_ref, given_ref):
-    heads, across, rows, size = along_ref.shape
+    outer, across, inner, rows, size = along_ref.shape
+    heads = outer * inner
     own_x, odd, time = lax.axis_index(ACROSS), lax.axis_index("core") == 1, own_time()
     later = jnp.minimum(own_x + 1, across - 1)
     step = step_size(times_ref, time)
@@ -126,14 +130,14 @@
         own = own_ref[:, columns]
         earlier = jnp.zeros((rows, size), jnp.float32)
         for source in range(across - 1):
-            term = along_ref[head, source].astype(jnp.float32)
+            term = along_ref[head // inner, source, head % inner].astype(jnp.float32)
             earlier = earlier + jnp.where(source < own_x, term, 0.0)
-        drift = (step * modulation_ref[2, :, columns]) * along_ref[head, own_x].astype(jnp.float32)
+        drift = (step * modulation_ref[2, :, columns]) * along_ref[head // inner, own_x, head % inner].astype(jnp.float32)
         first = jnp.where(time == 0, own.astype(jnp.float32), 0.0)
         upto = earlier + (drift + first)
         upto_ref[:, columns] = upto
         given_ref[:rows, columns] = jnp.where(odd, earlier, upto).astype(jnp.bfloat16)
-        given_ref[rows:, columns] = jnp.where(odd, own, along_ref[head, later])
+        given_ref[rows:, columns] = jnp.where(odd, own, along_ref[head // inner, later, head % inner])
 
 
 def finish_kernel(upto_ref, pairs_ref, end_ref, new_ref, error_ref):
@@ -190,14 +194,14 @@
     tokens = lax.all_to_all(sent.reshape(group, rows, size), ORDER, 0, 0, tiled=True)
     sent = call(
         functools.partial(attend_kernel, 256),
-        low(heads, across, rows, size),
+        low(heads // 4, across, 4, rows, size),
         tokens.reshape(heads // AFTER, copies, AFTER * rows, size),
         timesteps,
         modulation,
         weights,
     )
     along = lax.all_to_all(
-        sent.reshape(across * heads, rows, size), NEAR + ACROSS, 0, 0, tiled=True
+        sent.reshape(across * heads, rows, size), NEAR[:3] + ACROSS + NEAR[3:], 0, 0, tiled=True
     )
     upto, given = call(
         gather_kernel,
@@ -205,7 +209,7 @@
         timesteps,
         modulation,
         own_latent,
-        along.reshape(heads, across, rows, size),
+        along.reshape(heads // 4, across, 4, rows, size),
     )
     pairs = lax.all_gather(given, "core")
     new, error = call(finish_kernel, [low(rows, width), wide(1, rows)], upto, pairs, end_latent)

time: 63 us -> 62.8 us (level)
    all_gather x1, blocking collectives: 5.96 us -> 5.18 us  [body(): pairs = lax.all_gather(given, 'core')]
where the time goes in v6:
time: 62.8 us; the launch traced here: 62.6 us
  blocking collectives  58.7 us (93%)
  Pallas kernels  3.25 us (5%)
  between operations  0.65 us (1%)
    all_to_all x1, blocking collectives, body(): lax.all_to_all(sent.reshape(group, rows, size), ORDER, 0, 0, tiled=True)  28.8 us
    all_to_all x1, blocking collectives, body(): lax.all_to_all(sent.reshape(across * heads, rows, size), NEAR[:3] + ACROS...  24.7 us
    all_gather x1, blocking collectives, body(): pairs = lax.all_gather(given, 'core')  5.18 us
    pallas_call x4, Pallas kernels, call(): pl.pallas_call(kernel, out_shape=shapes, in_specs=[VMEM] * len(operands)...  3.25 us

profile of v6, /device:TPU:1, one launch (start us, length us, event | category | flops | bytes accessed | tf_op | source)
XLA Modules:
  0.0 62.6 jit_solution(11242613936524626161)
XLA Ops:
  0.6 1.1 %shard_map.68 = (bf16[1,2,32,16,128]{4,3,2,1,0:T(8,128)(2,1)S(1)}, bf16[16,4096]{1,0:T(8,128)(2,1)S(1)}, bf16[3,128,128]{2,1,0:T(8,128)(2,1)S(1)}, f32[3,1,4096]...) custom-call(bf16[16,4096]{1,0:T(8,128)(2,1)} %bitcast.14, bf16[3,32,128,128]{3,2,1,0:T(8,128)(2,1)} %weights_hbm.1, ...), custom_call_target="tpu_custom_call" | custom-call | tf_op jit(solution)/shard_map/pallas_call | solution.py:16
  1.7 28.8 %all_to_all.10 = bf16[64,16,128]{2,1,0:T(8,128)(2,1)S(1)} all-to-all(bf16[64,16,128]{2,1,0:T(8,128)(2,1)S(1)} %bitcast.13), channel_id=1, replica_groups=mesh['x1'=2,'x0'=2,'core'=2,'y2'=2,'y1'=2,'y0'=2,'z2'=2,'z1'=2,'z0'=2] {..., dimensions={0} | all-to-all | bytes 524288 | tf_op jit(solution)/shard_map/all_to_all | solution.py:194
  30.6 1.2 %shard_map.69 = bf16[8,4,4,16,128]{4,3,2,1,0:T(8,128)(2,1)S(1)} custom-call(bf16[1,2,512,128]{3,2,1,0:T(8,128)(2,1)S(1)} %bitcast.12, s32[1,9]{1,0:T(1,128)S(1)} %get-tuple-element.12.times_ref, f32[3,1,4096]{2,1,0:T(1,128)S(1)} %get-tuple-element.13.modulation_ref, bf16[3,128,128]{2,1,0:T(8,128)(2,1)S(1)} %get-tuple-element.16.weights_ref), custom_call_target="tpu_custom_call" | custom-call | tf_op jit(solution)/shard_map/pallas_call | solution.py:16
  31.8 24.7 %all_to_all.11 = bf16[128,16,128]{2,1,0:T(8,128)(2,1)S(1)} all-to-all(bf16[128,16,128]{2,1,0:T(8,128)(2,1)S(1)} %bitcast.11), channel_id=1, replica_groups=mesh['x1'=2,'x0'=2,'core'=2,'y2'=2,'y1'=2,'y0'=2,'z2'=2,'z1'=2,'z0'=2] {..., dimensions={0} | all-to-all | bytes 1048576 | tf_op jit(solution)/shard_map/all_to_all | solution.py:203
  56.5 0.2 shard_map.70
  56.7 5.2 %all-gather = bf16[64,4096]{1,0:T(8,128)(2,1)S(1)} all-gather(bf16[32,4096]{1,0:T(8,128)(2,1)S(1)} %get-tuple-element.18), channel_id=2, replica_groups=mesh['x1'=2,'x0'=2,'core'=2,'y2'=2,'y1'=2,'y0'=2,'z2'=2,'z1'=2,'z0'=2] {..., dimensions={0}, use_global_device_ids=true | all-gather | bytes 786432 | tf_op jit(solution)/shard_map/all_gather | solution.py:214
  61.8 0.7 %shard_map.71 = (bf16[16,4096]{1,0:T(8,128)(2,1)}, f32[1,16]{1,0:T(1,128)}) custom-call(f32[16,4096]{1,0:T(8,128)S(1)} %get-tuple-element.17.upto_ref, bf16[2,32,4096]{2,1,0:T(8,128)(2,1)S(1)} %bitcast.9, bf16[16,4096]{1,0:T(8,128)(2,1)S(1)} %get-tuple-element.19.end_ref), custom_call_target="tpu_custom_call" | custom-call | tf_op jit(solution)/shard_map/pallas_call | solution.py:16

commit v7 on v6

--- a/solution.py
+++ b/solution.py
@@ -49,24 +49,29 @@
     *done,
 ):
     before, copies, after, _, size = sent_ref.shape
+    width = own_ref.shape[1] // 4
+    pieces = [slice(start, start + width) for start in range(0, 4 * width, width)]
     fetches = [
+        pltpu.make_async_copy(latent_hbm.at[:, piece], own_ref.at[:, piece], semaphore)
+        for piece, semaphore in zip(pieces, done[4:])
+    ] + [
         pltpu.make_async_copy(source, target, semaphore)
         for source, target, semaphore in (
-            (latent_hbm, own_ref, done[0]),
-            (weights_hbm.at[:, lax.axis_index(NEAR)], weights_ref, done[1]),
-            (modulation_hbm, modulation_ref, done[2]),
-            (times_hbm, times_ref, done[3]),
-            (end_hbm, end_ref, done[4]),
+            (weights_hbm.at[:, lax.axis_index(NEAR)], weights_ref, done[0]),
+            (modulation_hbm, modulation_ref, done[1]),
+            (times_hbm, times_ref, done[2]),
+            (end_hbm, end_ref, done[3]),
         )
     ]
     for fetch in fetches:
         fetch.start()
-    fetches[0].wait()
     for head in range(before * after):
+        if head * size % width == 0:
+            fetches[head * size // width].wait()
         block = own_ref[:, head * size : (head + 1) * size]
         for copy in range(copies):
             sent_ref[head // after, copy, head % after] = block
-    for fetch in fetches[1:]:
+    for fetch in fetches[4:]:
         fetch.wait()
 
 
@@ -189,7 +194,7 @@
         ],
         *(pltpu.with_memory_space_constraint(operand, pltpu.HBM) for operand in inputs),
         specs=[HBM] * len(inputs),
-        scratch=[pltpu.SemaphoreType.DMA] * len(inputs),
+        scratch=[pltpu.SemaphoreType.DMA] * (len(inputs) + 3),
     )
     tokens = lax.all_to_all(sent.reshape(group, rows, size), ORDER, 0, 0, tiled=True)
     sent = call(

time: 62.8 us -> 62.8 us (level)
  no operation moved by 1% of the time
where the time goes in v7:
time: 62.8 us; the launch traced here: 62.6 us
  blocking collectives  58.7 us (93%)
  Pallas kernels  3.29 us (5%)
  between operations  0.65 us (1%)
    all_to_all x1, blocking collectives, body(): lax.all_to_all(sent.reshape(group, rows, size), ORDER, 0, 0, tiled=True)  28.8 us
    all_to_all x1, blocking collectives, body(): lax.all_to_all(sent.reshape(across * heads, rows, size), NEAR[:3] + ACROS...  24.7 us
    all_gather x1, blocking collectives, body(): pairs = lax.all_gather(given, 'core')  5.18 us
    pallas_call x4, Pallas kernels, call(): pl.pallas_call(kernel, out_shape=shapes, in_specs=[VMEM] * len(operands)...  3.29 us

profile of v7, /device:TPU:1, one launch (start us, length us, event | category | flops | bytes accessed | tf_op | source)
XLA Modules:
  0.0 62.6 jit_solution(2890709066892356065)
XLA Ops:
  0.6 1.1 %shard_map.68 = (bf16[1,2,32,16,128]{4,3,2,1,0:T(8,128)(2,1)S(1)}, bf16[16,4096]{1,0:T(8,128)(2,1)S(1)}, bf16[3,128,128]{2,1,0:T(8,128)(2,1)S(1)}, f32[3,1,4096]...) custom-call(bf16[16,4096]{1,0:T(8,128)(2,1)} %bitcast.14, bf16[3,32,128,128]{3,2,1,0:T(8,128)(2,1)} %weights_hbm.1, ...), custom_call_target="tpu_custom_call" | custom-call | tf_op jit(solution)/shard_map/pallas_call | solution.py:16
  1.8 28.8 %all_to_all.10 = bf16[64,16,128]{2,1,0:T(8,128)(2,1)S(1)} all-to-all(bf16[64,16,128]{2,1,0:T(8,128)(2,1)S(1)} %bitcast.13), channel_id=1, replica_groups=mesh['x1'=2,'x0'=2,'core'=2,'y2'=2,'y1'=2,'y0'=2,'z2'=2,'z1'=2,'z0'=2] {..., dimensions={0} | all-to-all | bytes 524288 | tf_op jit(solution)/shard_map/all_to_all | solution.py:199
  30.6 1.2 %shard_map.69 = bf16[8,4,4,16,128]{4,3,2,1,0:T(8,128)(2,1)S(1)} custom-call(bf16[1,2,512,128]{3,2,1,0:T(8,128)(2,1)S(1)} %bitcast.12, s32[1,9]{1,0:T(1,128)S(1)} %get-tuple-element.12.times_ref, f32[3,1,4096]{2,1,0:T(1,128)S(1)} %get-tuple-element.13.modulation_ref, bf16[3,128,128]{2,1,0:T(8,128)(2,1)S(1)} %get-tuple-element.16.weights_ref), custom_call_target="tpu_custom_call" | custom-call | tf_op jit(solution)/shard_map/pallas_call | solution.py:16
  31.8 24.7 %all_to_all.11 = bf16[128,16,128]{2,1,0:T(8,128)(2,1)S(1)} all-to-all(bf16[128,16,128]{2,1,0:T(8,128)(2,1)S(1)} %bitcast.11), channel_id=1, replica_groups=mesh['x1'=2,'x0'=2,'core'=2,'y2'=2,'y1'=2,'y0'=2,'z2'=2,'z1'=2,'z0'=2] {..., dimensions={0} | all-to-all | bytes 1048576 | tf_op jit(solution)/shard_map/all_to_all | solution.py:208
  56.5 0.2 shard_map.70
  56.7 5.2 %all-gather = bf16[64,4096]{1,0:T(8,128)(2,1)S(1)} all-gather(bf16[32,4096]{1,0:T(8,128)(2,1)S(1)} %get-tuple-element.18), channel_id=2, replica_groups=mesh['x1'=2,'x0'=2,'core'=2,'y2'=2,'y1'=2,'y0'=2,'z2'=2,'z1'=2,'z0'=2] {..., dimensions={0}, use_global_device_ids=true | all-gather | bytes 786432 | tf_op jit(solution)/shard_map/all_gather | solution.py:219
  61.9 0.7 %shard_map.71 = (bf16[16,4096]{1,0:T(8,128)(2,1)}, f32[1,16]{1,0:T(1,128)}) custom-call(f32[16,4096]{1,0:T(8,128)S(1)} %get-tuple-element.17.upto_ref, bf16[2,32,4096]{2,1,0:T(8,128)(2,1)S(1)} %bitcast.9, bf16[16,4096]{1,0:T(8,128)(2,1)S(1)} %get-tuple-element.19.end_ref), custom_call_target="tpu_custom_call" | custom-call | tf_op jit(solution)/shard_map/pallas_call | solution.py:16
